TPU v7x, 256 devices: a whole 4x4x8 slice. The times are simulated.
256 devices in a mesh: va: 8 (over z_hi, y), vb: 4 (over z_lo), oj: 8 (over x, core).
Axes of the slice: x: 4, y: 4, z: 8 (z_hi: 2, z_lo: 4; z = z_hi * 4 + z_lo), core: 2. Of those that a mesh axis runs over, the one named last changes fastest.
Arguments:
- occ_slab: bfloat16 [3584, 2, 2048], P(('vb', 'oj'), None, 'va'), may hold values from -0.875 to 0.875
- pair_slab: bfloat16 [3584, 8, 2048], P(('va', 'oj'), None, 'vb'), may hold values from -0.875 to 0.875
- occ_energy: float32 [2], replicated, may hold values from -1.5 to -0.3
- pair_energy: float32 [8], P('oj'), may hold values from -1.5 to -0.3
- vir_energy: float32 [2048], replicated, may hold values from 0.2 to 3
Outputs:
- gamma_occ: float32 [3584, 2, 2048], P(('vb', 'oj'), None, 'va')
- gamma_pair: float32 [3584, 8, 2048], P('va', 'oj', 'vb')
All inputs are finite; a program needn't handle non-finite values.
Results may differ from a plain program's by a relative error of at most 0.002.
Values may be sent and summed in bfloat16 or wider, within the bound.
A program may use at most 128 MiB of HBM per device.

v0:
```python
import jax
import jax.numpy as jnp
from jax import lax
from jax.sharding import PartitionSpec as P


def per_device(occ_slab, pair_slab, occ_energy, pair_energy, vir_energy):
    occ_full = lax.all_gather(occ_slab, ("vb", "oj"), axis=0, tiled=True)
    collected = lax.all_gather(pair_slab, "va", axis=0, tiled=True)
    mingled = lax.all_to_all(collected, "oj", split_axis=1, concat_axis=0, tiled=True)
    va_count = lax.axis_size("va")
    oj_count = lax.axis_size("oj")
    shaped = mingled.reshape(oj_count, va_count, -1, mingled.shape[1], mingled.shape[2])
    pair_full = jnp.swapaxes(shaped, 0, 1).reshape(-1, mingled.shape[1], mingled.shape[2])
    width_a = occ_full.shape[2]
    width_b = pair_full.shape[2]
    energy_a = lax.dynamic_slice_in_dim(vir_energy, lax.axis_index("va") * width_a, width_a)
    energy_b = lax.dynamic_slice_in_dim(vir_energy, lax.axis_index("vb") * width_b, width_b)
    pair_ints = jnp.einsum("qia,qjb->ijab", occ_full, pair_full, preferred_element_type=jnp.float32)
    denominator = (
        occ_energy[:, None, None, None]
        + pair_energy[None, :, None, None]
        - energy_a[None, None, :, None]
        - energy_b[None, None, None, :]
    )
    amplitudes = (pair_ints / denominator).astype(jnp.bfloat16)
    gamma_occ = lax.psum_scatter(
        jnp.einsum("ijab,qjb->qia", amplitudes, pair_full, preferred_element_type=jnp.float32),
        ("vb", "oj"),
        scatter_dimension=0,
        tiled=True,
    )
    gamma_pair = lax.psum_scatter(
        jnp.einsum("ijab,qia->qjb", amplitudes, occ_full, preferred_element_type=jnp.float32),
        "va",
        scatter_dimension=0,
        tiled=True,
    )
    return (gamma_occ, gamma_pair)


def solution(mesh):
    placed = (P(("vb", "oj"), None, "va"), P(("va", "oj"), None, "vb"), P(), P("oj"), P())
    return jax.shard_map(
        per_device,
        mesh=mesh,
        in_specs=placed,
        out_specs=(P(("vb", "oj"), None, "va"), P("va", "oj", "vb")),
        check_vma=False,
    )
```

profile of v0, /device:TPU:1, one launch (start us, length us, event | category | flops | bytes accessed | tf_op | source)
XLA Modules:
  0.0 833.1 jit_solution(16251034097933430811)
XLA Ops:
  7.2 0.0 all-gather.3.cloned.1.call-start
  7.2 1.9 copy.25
  9.1 0.0 all-gather.3.cloned.1.call-update
  9.2 0.0 all-gather.5.cloned.1.call-start
  9.2 1.6 copy.27
  10.8 0.0 all-gather.5.cloned.1.call-update
  10.8 0.0 copy-start.1
  10.8 103.1 %all-gather.3.cloned.1.call-done = bf16[448,8,512]{2,0,1:T(8,128)(2,1)} async-done(((bf16[56,8,512]{2,0,1:T(8,128)(2,1)}), bf16[448,8,512]{2,0,1:T(8,128)(2,1)}) %all-gather.3.cloned.1.call-update) | async-done | bytes 3670032 | tf_op jit(solution)/shard_map/all_gather | solution.py:9
  113.9 5.5 all-to-all-start
  119.4 0.0 all-reduce.7.cloned.1.call-start
  120.1 0.8 dynamic_slice.6
  120.8 0.8 dynamic_slice.7
  121.6 0.0 copy-done.1
  121.6 0.1 broadcast_subtract_fusion
  121.7 55.0 %all-to-all-done = bf16[448,8,512]{2,0,1:T(8,128)(2,1)} async-done(((bf16[448,8,512]{2,0,1:T(8,128)(2,1)}), bf16[448,8,512]{2,0,1:T(8,128)(2,1)}, u32[]{:S(2)}, u32[]{:S(2)}) %all-to-all-start) | async-done | bytes 3670048 | tf_op jit(solution)/shard_map/all_to_all | solution.py:10
  176.7 4.2 copy.26
  180.9 11.5 %all-gather.5.cloned.1.call-done = bf16[3584,2,256]{2,0,1:T(8,128)(2,1)} async-done(((bf16[112,2,256]{2,0,1:T(8,128)(2,1)}), bf16[3584,2,256]{2,0,1:T(8,128)(2,1)}) %all-gather.5.cloned.1.call-update) | async-done | bytes 3670032 | tf_op jit(solution)/shard_map/all_gather | solution.py:8
  192.5 0.0 copy-start
  192.5 5.4 fusion.2
  197.9 0.0 copy-done
  197.9 5.1 convolution_bitcast_fusion
  203.0 16.6 %copy.31 = f32[3584,1,512]{2,1,0:T(1,128)} copy(f32[3584,1,512]{0,2,1:T(8,128)} %convolution_bitcast_fusion) | data formatting | bytes 14680064 | tf_op jit(solution)/shard_map/ijab,qia->qjb/dot_general | solution.py:34
  219.6 0.0 all-reduce.7.cloned.1.call-update
  219.7 0.0 all-reduce.5.cloned.1.call-start
  219.7 7.1 convolution_bitcast_fusion.1
  226.8 11.7 %copy.30 = f32[3584,2,256]{2,1,0:T(2,128)} copy(f32[3584,2,256]{0,2,1:T(8,128)} %convolution_bitcast_fusion.1) | data formatting | bytes 14680064 | tf_op jit(solution)/shard_map/ijab,qjb->qia/dot_general | solution.py:28
  238.6 0.0 copy-start.3
  238.6 0.0 copy-start.2
  238.6 0.0 all-reduce.5.cloned.1.call-update
  238.6 0.6 copy-done.3
  239.2 0.6 dynamic-slice.2
  239.8 0.0 copy-done.2
  239.8 0.6 dynamic-slice
  241.7 289.5 %all-reduce.7.cloned.1.call-done = f32[3584,1,512]{2,1,0:T(1,128)} async-done(((f32[3584,1,512]{2,1,0:T(1,128)}), f32[3584,1,512]{2,1,0:T(1,128)}) %all-reduce.7.cloned.1.call-update) | async-done | bytes 7340048
  531.2 2.7 constant_dynamic-slice_fusion
  533.9 291.0 %all-reduce.5.cloned.1.call-done = f32[3584,2,256]{2,1,0:T(2,128)} async-done(((f32[3584,2,256]{2,1,0:T(2,128)}), f32[3584,2,256]{2,1,0:T(2,128)}) %all-reduce.5.cloned.1.call-update) | async-done | bytes 7340048
  824.9 1.6 constant_dynamic-slice_fusion.1
  (1 shorter events, 0.0 us)
Async XLA Ops:
  7.2 106.8 %all-gather.3.cloned.1.call-start = ((), (), s32[]{:S(2)}) async-start(), calls=%async_computation.1 | async-start | bytes 4128768 | tf_op jit(solution)/shard_map/all_gather | solution.py:9
  9.2 183.3 %all-gather.5.cloned.1.call-start = ((), (), s32[]{:S(2)}) async-start(), calls=%async_computation.2 | async-start | bytes 3784704 | tf_op jit(solution)/shard_map/all_gather | solution.py:8
  10.8 110.8 %copy-start.1 = (f32[2]{0:T(128)S(1)}, f32[2]{0:T(128)}, u32[]{:S(2)}) copy-start(f32[2]{0:T(128)} %param.7) | copy-start | bytes 28
  113.9 62.8 %all-to-all-start = ((bf16[448,8,512]{2,0,1:T(8,128)(2,1)}), bf16[448,8,512]{2,0,1:T(8,128)(2,1)}, u32[]{:S(2)}, u32[]{:S(2)}) async-start(bf16[448,8,512]{2,0,1:T(8,128)(2,1)} %all-gather.3.cloned.1.call-done), calls=%async_computation | async-start | bytes 7340032 | tf_op jit(solution)/shard_map/all_to_all | solution.py:10
  119.4 411.8 %all-reduce.7.cloned.1.call-start = ((), (), s32[]{:S(2)}) async-start(), calls=%async_computation.4 | async-start | bytes 14680064
  192.5 5.4 copy-start
  219.7 605.3 %all-reduce.5.cloned.1.call-start = ((), (), s32[]{:S(2)}) async-start(), calls=%async_computation.3 | async-start | bytes 14680064
  238.6 0.7 copy-start.3
  238.6 1.3 copy-start.2
Sparse Core Ops, SparseCore 0:
  11.1 102.7 all-gather.2
  116.3 76.1 all-gather.4
  219.8 311.3 all-reduce.6
  533.7 291.1 all-reduce.4
where the time goes:
time: 834 us; the launch traced here: 833 us
  waiting for transfers between devices  750 us (90%)
  local copies, waits for them, and re-layouts  43.8 us (5%)
  matrix products  17.6 us (2%)
  between operations  15.7 us (2%)
    unnamed x6, waiting for transfers between devices  581 us
    all_gather x1, waiting for transfers between devices, per_device(): collected = lax.all_gather(pair_slab, 'va', axis=0, tiled=True)  103 us
    all_to_all x1, waiting for transfers between devices, per_device(): lax.all_to_all(collected, 'oj', split_axis=1, concat_axis=0, tiled=True)  55 us
  transfers between devices with their start and end apart: 5, of which 5 were waited for; matrix products, arithmetic and copies ran while one was open for 4% of the time, Pallas kernels for 0%

commit v1 on v0

--- a/solution.py
+++ b/solution.py
@@ -7,7 +7,10 @@
 def per_device(occ_slab, pair_slab, occ_energy, pair_energy, vir_energy):
     occ_full = lax.all_gather(occ_slab, ("vb", "oj"), axis=0, tiled=True)
     collected = lax.all_gather(pair_slab, "va", axis=0, tiled=True)
-    mingled = lax.all_to_all(collected, "oj", split_axis=1, concat_axis=0, tiled=True)
+    peers = lax.axis_size("oj")
+    parts = jnp.stack(jnp.split(collected, peers, axis=1), axis=0)
+    parts = lax.all_to_all(parts, "oj", split_axis=0, concat_axis=0)
+    mingled = jnp.concatenate(parts, axis=0)
     va_count = lax.axis_size("va")
     oj_count = lax.axis_size("oj")
     shaped = mingled.reshape(oj_count, va_count, -1, mingled.shape[1], mingled.shape[2])

time: 834 us -> 696 us (0.83)
  waiting for transfers between devices: 750 us -> 605 us
    unnamed x6 -> x5, waiting for transfers between devices: 581 us -> 305 us
    reduce_scatter x0 -> x1, waiting for transfers between devices: none -> 144 us  [per_device(): lax.psum_scatter(jnp.einsum('ijab,qjb->qia', amplitudes, pair_full, prefe...]
    unnamed x14 -> x18, local copies, waits for them, and re-layouts: 9.68 us -> 22.1 us
    dot_general x1 -> x0, local copies, waits for them, and re-layouts: 11.7 us -> none  [per_device(): jnp.einsum('ijab,qjb->qia', amplitudes, pair_full, preferred_element_type...]
    all_gather x1, waiting for transfers between devices: 11.5 us -> 0.01 us  [per_device(): occ_full = lax.all_gather(occ_slab, ('vb', 'oj'), axis=0, tiled=True)]
  transfers between devices with their start and end apart: 5 -> 5, of which waited for: 5 -> 4; matrix products, arithmetic and copies ran while one was open for 4% -> 5% of each run, Pallas kernels for 0% -> 0%
where the time goes in v1:
time: 696 us; the launch traced here: 690 us
  waiting for transfers between devices  605 us (87%)
  local copies, waits for them, and re-layouts  46.4 us (7%)
  matrix products  17.5 us (3%)
  between operations  15.1 us (2%)
    unnamed x5, waiting for transfers between devices  305 us
    reduce_scatter x1, waiting for transfers between devices, per_device(): lax.psum_scatter(jnp.einsum('ijab,qjb->qia', amplitudes, pair_full, prefe...  144 us
    all_gather x1, waiting for transfers between devices, per_device(): collected = lax.all_gather(pair_slab, 'va', axis=0, tiled=True)  103 us
    all_to_all x1, waiting for transfers between devices, per_device(): parts = lax.all_to_all(parts, 'oj', split_axis=0, concat_axis=0)  53.4 us
    unnamed x18, local copies, waits for them, and re-layouts  22.1 us
    dot_general x1, local copies, waits for them, and re-layouts, per_device(): jnp.einsum('ijab,qia->qjb', amplitudes, occ_full, preferred_element_type=...  16.6 us
  transfers between devices with their start and end apart: 5, of which 4 were waited for; matrix products, arithmetic and copies ran while one was open for 5% of the time, Pallas kernels for 0%

profile of v1, /device:TPU:1, one launch (start us, length us, event | category | flops | bytes accessed | tf_op | source)
XLA Modules:
  0.0 689.9 jit_solution(5624880349592561552)
XLA Ops:
  7.2 0.0 all-gather.3.cloned.1.call-start
  7.2 1.9 copy.27
  9.1 0.0 all-gather.3.cloned.1.call-update
  9.2 0.0 all-gather.5.cloned.1.call-start
  9.2 1.6 copy.29
  10.8 0.0 all-gather.5.cloned.1.call-update
  10.8 103.2 %all-gather.3.cloned.1.call-done = bf16[448,8,512]{2,0,1:T(8,128)(2,1)} async-done(((bf16[56,8,512]{2,0,1:T(8,128)(2,1)}), bf16[448,8,512]{2,0,1:T(8,128)(2,1)}) %all-gather.3.cloned.1.call-update) | async-done | bytes 3670032 | tf_op jit(solution)/shard_map/all_gather | solution.py:9
  113.9 1.8 fusion.10
  115.8 1.9 fusion.9
  117.6 1.9 fusion.8
  119.5 1.9 fusion.7
  121.4 1.8 fusion.6
  123.2 1.8 fusion.5
  125.0 1.8 fusion.4
  126.8 1.8 fusion.3
  128.7 0.0 copy-start.1
  128.7 5.6 all-to-all-start
  134.3 0.0 all-reduce.3.cloned.1.call-start
  134.3 0.8 dynamic_slice.7
  135.0 0.8 dynamic_slice.6
  136.4 0.0 copy-done.1
  136.5 0.1 broadcast_subtract_fusion
  136.5 53.4 %all-to-all-done = bf16[8,448,1,512]{3,1,2,0:T(8,128)(2,1)} async-done(((bf16[8,448,1,512]{3,1,2,0:T(8,128)(2,1)}), bf16[8,448,1,512]{3,1,2,0:T(8,128)(2,1)}, u32[]{:S(2)}, u32[]{:S(2)}) %all-to-all-start) | async-done | bytes 3670048 | tf_op jit(solution)/shard_map/all_to_all | solution.py:12
  189.9 4.3 copy.28
  194.2 0.0 all-gather.5.cloned.1.call-done
  194.2 0.0 copy-start
  194.2 5.4 fusion.2
  199.6 0.0 copy-done
  199.6 5.1 convolution_bitcast_fusion
  204.7 16.6 %copy.32 = f32[3584,1,512]{2,1,0:T(1,128)} copy(f32[3584,1,512]{0,2,1:T(8,128)} %convolution_bitcast_fusion) | data formatting | bytes 14680064 | tf_op jit(solution)/shard_map/ijab,qia->qjb/dot_general | solution.py:37
  221.4 0.0 all-reduce.3.cloned.1.call-update
  221.4 0.0 reduce-scatter.2.cloned.1.call-start
  221.4 7.0 %fusion.11 = f32[3584,2,256]{2,0,1:T(8,128)} fusion(bf16[3584,512,1]{1,0,2:T(8,128)(2,1)} %bitcast.67, bf16[2,256,512]{1,2,0:T(8,128)(2,1)S(1)} %fusion.2), kind=kOutput, calls=%fused_computation.24 | convolution fusion | flops 1879048192 | bytes 11534336 | tf_op jit(solution)/shard_map/ijab,qjb->qia/dot_general | solution.py:31
  228.5 0.0 copy-start.2
  228.5 0.0 reduce-scatter.2.cloned.1.call-update
  228.5 0.6 copy-done.2
  229.1 0.6 dynamic-slice
  230.4 304.7 %all-reduce.3.cloned.1.call-done = f32[3584,1,512]{2,1,0:T(1,128)} async-done(((f32[3584,1,512]{2,1,0:T(1,128)}), f32[3584,1,512]{2,1,0:T(1,128)}) %all-reduce.3.cloned.1.call-update) | async-done | bytes 7340048
  535.0 2.7 constant_dynamic-slice_fusion
  537.8 143.8 %reduce-scatter.2.cloned.1.call-done = f32[112,2,256]{2,0,1:T(8,128)} async-done(((f32[3584,2,256]{2,0,1:T(8,128)}), f32[112,2,256]{2,0,1:T(8,128)}) %reduce-scatter.2.cloned.1.call-update) | async-done | bytes 229392 | tf_op jit(solution)/shard_map/reduce_scatter | solution.py:30
  681.5 1.8 copy.33
  (1 shorter events, 0.0 us)
Async XLA Ops:
  7.2 106.8 %all-gather.3.cloned.1.call-start = ((), (), s32[]{:S(2)}) async-start(), calls=%async_computation.2 | async-start | bytes 4128768 | tf_op jit(solution)/shard_map/all_gather | solution.py:9
  9.2 185.0 %all-gather.5.cloned.1.call-start = ((), (), s32[]{:S(2)}) async-start(), calls=%async_computation.3 | async-start | bytes 3784704 | tf_op jit(solution)/shard_map/all_gather | solution.py:8
  128.7 7.8 %copy-start.1 = (f32[2]{0:T(128)S(1)}, f32[2]{0:T(128)}, u32[]{:S(2)}) copy-start(f32[2]{0:T(128)} %param.7) | copy-start | bytes 28
  128.7 61.2 %all-to-all-start = ((bf16[8,448,1,512]{3,1,2,0:T(8,128)(2,1)}), bf16[8,448,1,512]{3,1,2,0:T(8,128)(2,1)}, u32[]{:S(2)}, u32[]{:S(2)}) async-start(bf16[8,448,1,512]{3,1,2,0:T(8,128)(2,1)} %fusion.3), calls=%async_computation | async-start | bytes 7340032 | tf_op jit(solution)/shard_map/all_to_all | solution.py:12
  134.3 400.8 %all-reduce.3.cloned.1.call-start = ((), (), s32[]{:S(2)}) async-start(), calls=%async_computation.5 | async-start | bytes 14680064
  194.2 5.4 copy-start
  221.4 460.1 %reduce-scatter.2.cloned.1.call-start = ((), (), s32[]{:S(2)}) async-start(), calls=%async_computation.4 | async-start | bytes 7569408 | tf_op jit(solution)/shard_map/reduce_scatter | solution.py:30
  228.5 0.7 copy-start.2
Sparse Core Ops, SparseCore 0:
  11.1 102.7 all-gather.2
  116.3 77.3 all-gather.4
  221.5 313.4 all-reduce.2
  537.5 144.0 reduce-scatter.1
